TPU v7x, 256 devices: a whole 4x4x8 slice. The times are simulated.
256 devices in a mesh: seq: 32 (over x, z), head: 8 (over y, core).
Axes of the slice: x: 4, y: 4, z: 8, core: 2. Of those that a mesh axis runs over, the one named last changes fastest.
Arguments:
- queries: bfloat16 [16384, 16, 128], P(('seq', 'head')), may hold values from -6 to 6
- key_vectors: bfloat16 [16384, 16, 128], P(('seq', 'head')), may hold values from -6 to 6
- value_vectors: bfloat16 [16384, 32, 128], P(('seq', 'head')), may hold values from -6 to 6
- output_gate: bfloat16 [16384, 32, 128], P(('seq', 'head')), may hold values from -6 to 6
- write_strength: bfloat16 [16384, 32], P(('seq', 'head'))
- norm_gain: bfloat16 [128], replicated, may hold values from 0.099609375 to 1.8984375
- output_weight: bfloat16 [4096, 2048], P('head'), may hold values from -0.09375 to 0.09375
Outputs:
- projected: bfloat16 [16384, 2048], P(('seq', 'head'))
All inputs are finite; a program needn't handle non-finite values.
Results may differ from a plain program's by a relative error of at most 0.017.
Values may be sent and summed in bfloat16 or wider, within the bound.
A program may use at most 128 MiB of HBM per device.

v0:
```python
import jax
import jax.numpy as jnp
from jax import lax
from jax.sharding import PartitionSpec as P

SPAN = 64


precise = lax.Precision.HIGHEST
epsilon = 1e-06


def prefix(value, axis, join, neutral):
    count, mine = (lax.axis_size(axis), lax.axis_index(axis))
    pieces = jax.tree.map(lambda part: lax.all_gather(part, axis), value)
    so_far = jax.tree.map(
        lambda part, zero: jnp.full_like(part, 0) + jnp.asarray(zero, part.dtype), value, neutral
    )

    def step(position, so_far):
        longer = join(so_far, jax.tree.map(lambda part: part[position], pieces))
        return jax.tree.map(lambda new, old: jnp.where(position < mine, new, old), longer, so_far)

    return lax.fori_loop(0, count - 1, step, so_far)


def unit_rows(values_in):
    return values_in * lax.rsqrt(jnp.sum(values_in * values_in, -1, keepdims=True) + epsilon)


def span_factors(key_blocks, value_blocks, strength_blocks):
    key_gram = jnp.einsum("...cd,...md->...cm", key_blocks, key_blocks, precision=precise)
    below_diagonal = jnp.tril(key_gram * strength_blocks[..., :, None], -1)
    block_size = key_blocks.shape[-2]
    system = below_diagonal + jnp.eye(block_size, dtype=key_blocks.dtype)
    right_sides = jnp.concatenate(
        [key_blocks * strength_blocks[..., None], value_blocks * strength_blocks[..., None]], -1
    )
    solved = jax.scipy.linalg.solve_triangular(system, right_sides, lower=True, unit_diagonal=True)
    head_width = key_blocks.shape[-1]
    return (solved[..., :head_width], solved[..., head_width:])


def span_step(carried, pieces):
    query_c, key_c, w_c, u_c = pieces
    scores = jnp.tril(jnp.einsum("...cd,...md->...cm", query_c, key_c, precision=precise))
    corrected = u_c - jnp.einsum("...cd,...de->...ce", w_c, carried, precision=precise)
    outputs = jnp.einsum("...cd,...de->...ce", query_c, carried, precision=precise) + jnp.einsum(
        "...cm,...me->...ce", scores, corrected, precision=precise
    )
    carried = carried + jnp.einsum("...cd,...ce->...de", key_c, corrected, precision=precise)
    return (carried, outputs)


def blocked(values_in):
    shard_rows, head_count, head_width = values_in.shape
    return jnp.transpose(
        values_in.reshape(shard_rows // SPAN, SPAN, head_count, head_width), (0, 2, 1, 3)
    )


def strength_blocked(values_in):
    shard_rows, head_count = values_in.shape
    return jnp.transpose(values_in.reshape(shard_rows // SPAN, SPAN, head_count), (0, 2, 1))


def compose(earlier_pair, later_pair):
    earlier_trans, earlier_state = earlier_pair
    later_trans, later_state = later_pair
    joined_trans = jnp.einsum("hde,hef->hdf", later_trans, earlier_trans, precision=precise)
    joined_state = (
        jnp.einsum("hde,hef->hdf", later_trans, earlier_state, precision=precise) + later_state
    )
    return (joined_trans, joined_state)


def per_device(
    queries, key_vectors, value_vectors, output_gate, write_strength, norm_gain, output_weight
):
    query_h, key_h, value_h, gate_h, strength_h = (
        lax.all_to_all(queries, "head", split_axis=1, concat_axis=0, tiled=True),
        lax.all_to_all(key_vectors, "head", split_axis=1, concat_axis=0, tiled=True),
        lax.all_to_all(value_vectors, "head", split_axis=1, concat_axis=0, tiled=True),
        lax.all_to_all(output_gate, "head", split_axis=1, concat_axis=0, tiled=True),
        lax.all_to_all(write_strength, "head", split_axis=1, concat_axis=0, tiled=True),
    )
    head_ratio = value_h.shape[1] // key_h.shape[1]
    head_width = value_h.shape[2]
    head_count = value_h.shape[1]
    shard_rows = value_h.shape[0]
    query_unit = jnp.repeat(
        unit_rows(query_h.astype(jnp.float32)) * head_width ** (-0.5), head_ratio, axis=1
    )
    key_unit = jnp.repeat(unit_rows(key_h.astype(jnp.float32)), head_ratio, axis=1)
    query_b = blocked(query_unit)
    key_b = blocked(key_unit)
    value_b = blocked(value_h.astype(jnp.float32))
    strength_b = strength_blocked(strength_h.astype(jnp.float32))
    w_b, u_b = span_factors(key_b, value_b, strength_b)
    identity = jnp.broadcast_to(
        jnp.eye(head_width, dtype=jnp.float32), (head_count, head_width, head_width)
    )
    empty_state = jnp.zeros((head_count, head_width, head_width), jnp.float32)

    def local_step(carried, pieces):
        transition, local_state = carried
        key_c, w_c, u_c = pieces
        span_trans = identity - jnp.einsum("hcd,hce->hde", key_c, w_c, precision=precise)
        local_state = jnp.einsum(
            "hde,hef->hdf", span_trans, local_state, precision=precise
        ) + jnp.einsum("hcd,hce->hde", key_c, u_c, precision=precise)
        transition = jnp.einsum("hde,hef->hdf", span_trans, transition, precision=precise)
        return ((transition, local_state), None)

    (transition, local_state), unused = lax.scan(
        local_step, (identity, empty_state), (key_b, w_b, u_b)
    )
    incoming = prefix((transition, local_state), "seq", compose, (identity, empty_state))
    final_state, outputs_b = lax.scan(span_step, incoming[1], (query_b, key_b, w_b, u_b))
    core = jnp.transpose(outputs_b, (0, 2, 1, 3)).reshape(shard_rows, head_count, head_width)
    mean_square = jnp.mean(core * core, -1, keepdims=True)
    normed = (
        core
        * lax.rsqrt(mean_square + epsilon)
        * norm_gain.astype(jnp.float32)
        * jax.nn.silu(gate_h.astype(jnp.float32))
    )
    gated = normed.astype(jnp.bfloat16)
    flat_rows = gated.reshape(shard_rows, head_count * head_width)
    return lax.psum_scatter(
        jnp.dot(flat_rows, output_weight, preferred_element_type=jnp.float32).astype(jnp.bfloat16),
        "head",
        scatter_dimension=0,
        tiled=True,
    )


def solution(mesh):
    placed = (
        P(("seq", "head"), None, None),
        P(("seq", "head"), None, None),
        P(("seq", "head"), None, None),
        P(("seq", "head"), None, None),
        P(("seq", "head"), None),
        P(),
        P("head", None),
    )
    return jax.shard_map(
        per_device, mesh=mesh, in_specs=placed, out_specs=P(("seq", "head"), None), check_vma=False
    )
```

profile of v0, /device:TPU:5, one launch (start us, length us, event | category | flops | bytes accessed | tf_op | source)
XLA Modules:
  0.0 567.1 jit_solution(8538602303684616108)
XLA Ops:
  8.1 5.1 all-to-all-start.1
  13.9 1.7 copy.57
  15.6 2.2 all-to-all-done.1
  17.8 4.0 all-to-all-start
  21.8 2.0 copy.61
  23.9 4.4 all-to-all-done
  28.3 5.1 all-to-all-start.2
  35.1 2.7 fusion.49
  37.9 158.7 %custom-call.4 = f32[8,4,1,64,64]{3,4,2,1,0:T(8,128)} custom-call(f32[8,4,1,64,64]{4,3,2,1,0:T(8,128)} %fusion.49), custom_call_target="InvertDiagBlocksLowerTriangular" | custom-call | tf_op jit(solution)/shard_map/jit(_solve_triangular)/vmap(vmap())/triangular_solve | solution.py:39
  198.1 2.0 fusion.41
  201.7 32.1 %while.40 = (s32[]{:T(128)}, f32[4,128,128]{2,1,0:T(8,128)S(1)}, f32[4,128,128]{2,1,0:T(8,128)S(1)}, f32[8,4,64,128]{3,2,1,0:T(8,128)}, f32[8,4,64,128]{3,2,1,0:...) while((s32[]{:T(128)}, f32[4,128,128]{2,1,0:T(8,128)S(1)}, ...), condition=%wide.region_2.3_spmd.clone, body=%wide.region_1.0_spmd.clone.sunk | while | flops 302186496 | bytes 3475559 | solution.py:115
  235.3 1.7 copy.63
  237.0 4.8 all-to-all-start.3
  242.9 5.5 all-to-all-done.3
  248.3 4.4 all-to-all-start.4
  254.0 2.0 fusion.59
  256.0 6.3 %all-to-all-done.4 = bf16[64,32,128]{2,0,1:T(8,128)(2,1)S(1)} async-done(((bf16[64,32,128]{2,0,1:T(8,128)(2,1)}), bf16[64,32,128]{2,0,1:T(8,128)(2,1)S(1)}, u32[]{:S(2)}, u32[]{:S(2)}) %all-to-all-start.4) | async-done | bytes 524320 | tf_op jit(solution)/shard_map/all_to_all | solution.py:84
  263.7 70.0 %all-gather.5.cloned.1.call-done = f32[128,128,128]{2,1,0:T(8,128)} async-done(((f32[4,128,128]{2,1,0:T(8,128)}), f32[128,128,128]{2,1,0:T(8,128)}) %all-gather.5.cloned.1.call-update) | async-done | bytes 8388624 | tf_op jit(solution)/shard_map/all_gather | solution.py:15
  333.7 98.0 %all-gather.7.cloned.1.call-done = f32[128,128,128]{2,1,0:T(8,128)} async-done(((f32[4,128,128]{2,1,0:T(8,128)}), f32[128,128,128]{2,1,0:T(8,128)}) %all-gather.7.cloned.1.call-update) | async-done | bytes 8388624 | tf_op jit(solution)/shard_map/all_gather | solution.py:15
  431.7 46.0 %while.41 = (s32[]{:T(128)}, f32[4,128,128]{2,1,0:T(8,128)S(1)}, s32[]{:T(128)}, f32[32,4,128,128]{3,2,1,0:T(8,128)}, f32[32,4,128,128]{3,2,1,0:T(8,128)}, /*index=5*/s32[]{:T(128)}, s32[]{:T(128)}) while((s32[]{:T(128)}, f32[4,128,128]{2,1,0:T(8,128)S(1)}, s32[]{:T(128)}, f32[32,4,128,128]{3,2,1,0:T(8,128)}, ...), condition=%wide.region_4.5_spmd.clone, body=%wide.region_3.4_spmd.clone.sunk | while | flops 100925440 | bytes 1837663 | solution.py:24
  478.7 43.5 %while.39 = (s32[]{:T(128)}, f32[4,128,128]{2,1,0:T(8,128)S(1)}, f32[8,4,64,128]{3,2,1,0:T(8,128)}, f32[8,4,64,128]{3,2,1,0:T(8,128)}, f32[8,4,64,128]{3,2,1,0:T...) while((s32[]{:T(128)}, f32[4,128,128]{2,1,0:T(8,128)S(1)}, ...), condition=%wide.region_7.8_spmd, body=%wide.region_6.7_spmd.sunk | while | flops 201478144 | bytes 2768469 | solution.py:119
  522.2 1.7 multiply_reduce_fusion
  525.4 2.6 convolution_convert_fusion
  528.1 32.5 %reduce-scatter.2.cloned.1.call-done = bf16[64,2048]{1,0:T(8,128)(2,1)} async-done(((bf16[512,2048]{1,0:T(8,128)(2,1)}), bf16[64,2048]{1,0:T(8,128)(2,1)}) %reduce-scatter.2.cloned.1.call-update) | async-done | bytes 262160 | tf_op jit(solution)/shard_map/reduce_scatter | solution.py:130
  (212 shorter events, 134.2 us)
Async XLA Ops:
  6.5 518.8 %copy-start = (bf16[512,2048]{1,0:T(8,128)(2,1)S(1)}, bf16[512,2048]{1,0:T(8,128)(2,1)}, u32[]{:S(2)}) copy-start(bf16[512,2048]{1,0:T(8,128)(2,1)} %param.19) | copy-start | bytes 6291460
  8.1 9.7 %all-to-all-start.1 = ((bf16[8,2,128]{2,1,0:T(2,128)(2,1)}), bf16[8,2,128]{2,1,0:T(2,128)(2,1)S(1)}, u32[]{:S(2)}, u32[]{:S(2)}) async-start(bf16[8,2,128]{2,1,0:T(2,128)(2,1)} %reshape.110), calls=%async_computation.1 | async-start | bytes 8192 | tf_op jit(solution)/shard_map/all_to_all | solution.py:85
  17.8 10.5 %all-to-all-start = ((bf16[64,16,128]{2,0,1:T(8,128)(2,1)}), bf16[64,16,128]{2,0,1:T(8,128)(2,1)S(1)}, u32[]{:S(2)}, u32[]{:S(2)}) async-start(bf16[64,16,128]{2,0,1:T(8,128)(2,1)} %copy.57), calls=%async_computation | async-start | bytes 524288 | tf_op jit(solution)/shard_map/all_to_all | solution.py:82
  28.3 168.3 %all-to-all-start.2 = ((bf16[64,32,128]{2,0,1:T(8,128)(2,1)}), bf16[64,32,128]{2,0,1:T(8,128)(2,1)}, u32[]{:S(2)}, u32[]{:S(2)}) async-start(bf16[64,32,128]{2,0,1:T(8,128)(2,1)} %copy.61), calls=%async_computation.2 | async-start | bytes 1048576 | tf_op jit(solution)/shard_map/all_to_all | solution.py:83
  33.4 300.3 %all-gather.5.cloned.1.call-start = ((), (), s32[]{:S(2)}) async-start(), calls=%async_computation.7 | async-start | bytes 8650752 | tf_op jit(solution)/shard_map/all_gather | solution.py:15
  34.0 1.2 copy-start.7
  196.6 1.5 copy-start.4
  201.7 40.1 %copy-start.6 = (bf16[64,32,128]{2,1,0:T(8,128)(2,1)S(1)}, bf16[64,32,128]{2,1,0:T(8,128)(2,1)}, u32[]{:S(2)}) copy-start(bf16[64,32,128]{2,1,0:T(8,128)(2,1)} %param.16) | copy-start | bytes 1572868
  233.8 0.7 copy-start.1
  233.8 0.8 copy-start.2
  233.8 9.0 %copy-start.8 = (bf16[128]{0:T(256)(128)(2,1)S(1)}, bf16[128]{0:T(256)(128)(2,1)}, u32[]{:S(2)}) copy-start(bf16[128]{0:T(256)(128)(2,1)} %param.18) | copy-start | bytes 772
  234.6 197.1 %all-gather.7.cloned.1.call-start = ((), (), s32[]{:S(2)}) async-start(), calls=%async_computation.8 | async-start | bytes 8650752 | tf_op jit(solution)/shard_map/all_gather | solution.py:15
  237.0 11.3 %all-to-all-start.3 = ((bf16[64,16,128]{2,0,1:T(8,128)(2,1)}), bf16[64,16,128]{2,0,1:T(8,128)(2,1)S(1)}, u32[]{:S(2)}, u32[]{:S(2)}) async-start(bf16[64,16,128]{2,0,1:T(8,128)(2,1)} %copy.63), calls=%async_computation.3 | async-start | bytes 524288 | tf_op jit(solution)/shard_map/all_to_all | solution.py:81
  248.3 13.9 %all-to-all-start.4 = ((bf16[64,32,128]{2,0,1:T(8,128)(2,1)}), bf16[64,32,128]{2,0,1:T(8,128)(2,1)S(1)}, u32[]{:S(2)}, u32[]{:S(2)}) async-start(bf16[64,32,128]{2,0,1:T(8,128)(2,1)} %copy.70), calls=%async_computation.4 | async-start | bytes 1048576 | tf_op jit(solution)/shard_map/all_to_all | solution.py:84
  252.8 307.7 %reduce-scatter.2.cloned.1.call-start = ((), (), s32[]{:S(2)}) async-start(), calls=%async_computation.6 | async-start | bytes 2359296 | tf_op jit(solution)/shard_map/reduce_scatter | solution.py:130
  522.2 1.9 copy-start.3
  524.1 1.3 copy-start.5
Sparse Core Ops, SparseCore 0:
  234.7 98.9 all-gather.4
  336.2 95.3 all-gather.6
  528.2 32.2 reduce-scatter.1
where the time goes:
time: 572 us; the launch traced here: 567 us
  waiting for transfers between devices  219 us (38%)
  other arithmetic  165 us (29%)
  matrix products  126 us (22%)
  starting transfers between devices  23.5 us (4%)
  local copies, waits for them, and re-layouts  17.3 us (3%)
  between operations  13.4 us (2%)
    all_gather x2, waiting for transfers between devices, prefix(): pieces = jax.tree.map(lambda part: lax.all_gather(part, axis), value)  168 us
    another operation x4, other arithmetic, span_factors(): jax.scipy.linalg.solve_triangular(system, right_sides, lower=True, unit_d...  159 us
    dot_general x31, matrix products, compose(): jnp.einsum('hde,hef->hdf', later_trans, earlier_state, precision=precise)  44.3 us
    reduce_scatter x1, waiting for transfers between devices, per_device(): lax.psum_scatter(jnp.dot(flat_rows, output_weight, preferred_element_type...  32.5 us
    dot_general x8, matrix products, local_step(): jnp.einsum('hcd,hce->hde', key_c, w_c, precision=precise)  12.6 us
    dot_general x8, matrix products, local_step(): jnp.einsum('hcd,hce->hde', key_c, u_c, precision=precise)  12.5 us
    dot_general x8, matrix products, span_step(): jnp.einsum('...cd,...ce->...de', key_c, corrected, precision=precise)  12.1 us
  transfers between devices with their start and end apart: 8, of which 7 were waited for; matrix products, arithmetic and copies ran while one was open for 31% of the time, Pallas kernels for 0%

commit v1 on v0

v1 whole, which is shorter than its diff:
```python
import functools

import jax
import jax.numpy as jnp
from jax import lax
from jax.experimental import pallas as pl
from jax.experimental.pallas import tpu as pltpu
from jax.sharding import PartitionSpec as P

F32 = jnp.float32
BF16 = jnp.bfloat16
MESH = pl.DeviceIdType.MESH
EPS = 1e-06
C = 128
ROWS = 64
NH = 8
NZ = 8
NX = 4
NY = 4
HV = 4
HK = 2
TOK = ROWS * NH
NB = TOK // C
DM = 2048
HALF = DM // 2
LEVELS = (2, 4, 8, 16, 32, 64)


def nn(a, b):
    return jnp.dot(a, b, preferred_element_type=F32)


def nt(a, b):
    return lax.dot_general(a, b, (((1,), (1,)), ((), ())), preferred_element_type=F32)


def tn(a, b):
    return lax.dot_general(a, b, (((0,), (0,)), ((), ())), preferred_element_type=F32)


def block_rows(c):
    return pl.ds(pl.multiple_of(c * C, C), C)


def kernel(
    q_hbm, k_hbm, v_hbm, g_hbm, b_hbm, gain_ref, w_hbm, out_ref,
    q_in, k_in, v_in, g_in, b_in, w_own, w_sib,
    q_f, k_f, v_f, g_f,
    q_send, k_send, v_send, g_send,
    q_recv, k_recv, v_recv, g_recv,
    masks, rk_row, rk_col, x_u, x_w, wu, chain, before,
    y_q, y_o, gate,
    x_send, x_recv, prefix, x_total, state, s_send, s_in,
    g_mine, g_sib, p_f, p_b, relay_a, relay_b, join_a, join_b,
    minus_a, minus_b, plus_a, plus_b,
    in_sem, own_sem, a2a_send, a2a_recv, w_send_sem, w_recv_sem,
    z_send, z_recv, t_send, t_recv, s_send_sem, s_recv,
    sib_send, sib_recv, rs_send, rs_recv,
):
    seq = lax.axis_index("seq")
    head = lax.axis_index("head")
    x = seq // NZ
    z = lax.rem(seq, NZ)
    y = head // 2
    core = lax.rem(head, 2)
    sibling = y * 2 + (1 - core)

    def on_head(h):
        return (seq, h)

    def on_z(zz):
        return (x * NZ + zz, head)

    def on_x(xx):
        return (xx * NZ + z, head)

    peers = [(2, 0), (2, 1), (1, 0), (1, 1), (3, 0), (3, 1), (0, 1)]

    def head_at(dy, dc):
        return lax.rem(y + dy, NY) * 2 + lax.rem(core + dc, 2)

    barrier = pltpu.get_barrier_semaphore()
    for dy, dc in peers:
        pl.semaphore_signal(barrier, inc=1, device_id=on_head(head_at(dy, dc)), device_id_type=MESH)
    for dz in range(1, NZ):
        pl.semaphore_signal(barrier, inc=1, device_id=on_z(lax.rem(z + dz, NZ)), device_id_type=MESH)
    for dx in range(1, NX):
        pl.semaphore_signal(barrier, inc=1, device_id=on_x(lax.rem(x + dx, NX)), device_id_type=MESH)

    loads = [
        pltpu.make_async_copy(src, dst, in_sem.at[i])
        for i, (src, dst) in enumerate(
            [(k_hbm, k_in), (b_hbm, b_in), (v_hbm, v_in), (q_hbm, q_in), (g_hbm, g_in), (w_hbm, w_own)]
        )
    ]
    for copy in loads:
        copy.start()

    ri = lax.broadcasted_iota(jnp.int32, (C, C), 0)
    ci = lax.broadcasted_iota(jnp.int32, (C, C), 1)
    for i, s in enumerate(LEVELS):
        keep = (ri // (2 * s) == ci // (2 * s)) & (ri // s != ci // s)
        masks[i] = jnp.where(keep, 1.0, 0.0).astype(BF16)

    def to_columns(raw, wide, send, heads):
        per = heads // NH
        wide[...] = raw[...].astype(F32)
        for h in range(heads):
            send[h // per, :, (h % per) * C : (h % per + 1) * C] = wide[
                pl.ds(h, ROWS, stride=heads), :
            ].astype(BF16)

    sends = [(k_send, k_recv), (v_send, v_recv), (q_send, q_recv), (g_send, g_recv)]

    def peer_copy(array, i):
        send, recv = sends[array]
        target = head_at(*peers[i])
        return pltpu.make_async_remote_copy(
            src_ref=send.at[target],
            dst_ref=recv.at[pl.ds(pl.multiple_of(head * ROWS, ROWS), ROWS), :],
            send_sem=a2a_send.at[array, i],
            recv_sem=a2a_recv.at[array, i],
            device_id=on_head(target),
            device_id_type=MESH,
        )

    def own_copy(array):
        send, recv = sends[array]
        return pltpu.make_async_copy(
            send.at[head], recv.at[pl.ds(pl.multiple_of(head * ROWS, ROWS), ROWS), :], own_sem.at[array]
        )

    def start_exchange(array):
        for i in range(len(peers)):
            peer_copy(array, i).start()
        own_copy(array).start()

    def wait_exchange(array):
        own_copy(array).wait()
        for i in range(len(peers)):
            peer_copy(array, i).wait_recv()

    loads[0].wait()
    loads[1].wait()
    to_columns(k_in, k_f, k_send, HK * NH)
    for h in range(NH):
        k_send[h, :, HK * C :] = jnp.zeros((ROWS, C), BF16)
        k_send[h, :, HK * C : HK * C + HV * NH] = b_in[...]
    pl.semaphore_wait(barrier, len(peers) + (NZ - 1) + (NX - 1))
    start_exchange(0)
    loads[2].wait()
    to_columns(v_in, v_f, v_send, HV * NH)
    start_exchange(1)
    loads[3].wait()
    to_columns(q_in, q_f, q_send, HK * NH)
    start_exchange(2)
    loads[4].wait()
    to_columns(g_in, g_f, g_send, HV * NH)
    start_exchange(3)
    weight_copy = pltpu.make_async_remote_copy(
        src_ref=w_hbm, dst_ref=w_sib, send_sem=w_send_sem, recv_sem=w_recv_sem,
        device_id=on_head(sibling), device_id_type=MESH,
    )
    weight_copy.start()

    wait_exchange(0)
    chains = 2

    def invert(step, carry):
        eye = ri == ci
        lower = ri > ci
        todo = []
        for part in range(chains):
            c = step * chains + part
            rows = block_rows(c)
            strengths = k_recv[rows, HK * C :].astype(F32)
            for j in range(HK):
                kb = k_recv[rows, j * C : (j + 1) * C]
                gram = nt(kb, kb)
                diag = jnp.where(eye, gram, 0.0)
                kc = lax.rsqrt(jnp.sum(diag, 1, keepdims=True) + EPS)
                kr = lax.rsqrt(jnp.sum(diag, 0, keepdims=True) + EPS)
                rk_row[j, c] = jnp.broadcast_to(kr, (8, C))
                rk_col[j, c] = jnp.broadcast_to(kc, (C, C))
                scaled = jnp.where(lower, gram * kc * kr, 0.0)
                for n in (2 * j, 2 * j + 1):
                    bc = jnp.sum(jnp.where(ci == head * HV + n, strengths, 0.0), 1, keepdims=True)
                    br = jnp.sum(jnp.where(eye, bc, 0.0), 0, keepdims=True)
                    a = scaled * bc
                    todo.append((n, c, a.astype(BF16), br, kr, jnp.where(eye, 1.0, jnp.where(ri // 2 == ci // 2, -a, 0.0))))
        xs = [t[5] for t in todo]
        for i in range(len(LEVELS)):
            xb = [xx.astype(BF16) for xx in xs]
            right = [nn(t[2] * masks[i], b).astype(BF16) for t, b in zip(todo, xb)]
            xs = [xx - nn(b, r) for xx, b, r in zip(xs, xb, right)]
        for (n, c, _, br, kr, _), xx in zip(todo, xs):
            x_u[n, c] = (xx * br).astype(BF16)
            x_w[n, c] = (xx * (br * kr)).astype(BF16)
        return carry

    lax.fori_loop(0, NB // chains, invert, 0)

    wait_exchange(1)
    chain[...] = jnp.zeros_like(chain)

    def advance(c, carry):
        rows = block_rows(c)
        keys = [k_recv[rows, j * C : (j + 1) * C] for j in range(HK)]
        cols = [rk_col[j, c] for j in range(HK)]
        ws = [nn(x_w[n, c], keys[n // 2]) for n in range(HV)]
        us = [nn(x_u[n, c], v_recv[rows, n * C : (n + 1) * C]) for n in range(HV)]
        scaled = []
        for n in range(HV):
            wu[n, c, :, :C] = ws[n].astype(BF16)
            wu[n, c, :, C:] = us[n].astype(BF16)
            scaled.append(
                jnp.concatenate([ws[n] * -cols[n // 2], us[n] * cols[n // 2]], 1).astype(BF16)
            )
        news = [tn(keys[n // 2], scaled[n]) for n in range(HV)]
        for n in range(HV):
            now = chain[n]
            now_b = now.astype(BF16)
            before[n, c] = now_b
            chain[n] = now + nn(news[n][:, :C].astype(BF16), now_b) + news[n]
        return carry

    lax.fori_loop(0, NB, advance, 0)
    for n in range(HV):
        x_send[n] = chain[n].astype(BF16)

    is_owner = lax.rem(z, 2) == core
    mine = z // 2

    def to_owner(n):
        return pltpu.make_async_remote_copy(
            src_ref=x_send.at[n], dst_ref=x_recv.at[z], send_sem=z_send.at[n], recv_sem=z_recv.at[z],
            device_id=on_z(2 * n + core), device_id_type=MESH,
        )

    def from_z(zz):
        return pltpu.make_async_remote_copy(
            src_ref=x_send.at[0], dst_ref=x_recv.at[zz], send_sem=z_send.at[0], recv_sem=z_recv.at[zz],
            device_id=on_z(zz), device_id_type=MESH,
        )

    for n in range(HV):
        @pl.when(z != 2 * n + core)
        def _():
            to_owner(n).start()

        @pl.when(z == 2 * n + core)
        def _():
            x_recv[z] = x_send[n]

    wait_exchange(2)

    def outputs(c, carry):
        rows = block_rows(c)
        for j in range(HK):
            qb = q_recv[rows, j * C : (j + 1) * C]
            kb = k_recv[rows, j * C : (j + 1) * C]
            qf = qb.astype(F32)
            qc = lax.rsqrt(jnp.sum(qf * qf, 1, keepdims=True) + EPS) * (C ** -0.5)
            scores = jnp.where(ri >= ci, nt(qb, kb) * qc * rk_row[j, c, 0:1, :], 0.0).astype(BF16)
            unit = qf * qc
            for n in (2 * j, 2 * j + 1):
                part = nn(scores, wu[n, c])
                eff = unit - part[:, :C]
                moved = nn(eff.astype(BF16), before[n, c])
                y_q[n, rows, :] = (eff + moved[:, :C]).astype(BF16)
                y_o[n, rows, :] = part[:, C:] + moved[:, C:]
        return carry

    lax.fori_loop(0, NB, outputs, 0)

    def to_x(dx):
        return pltpu.make_async_remote_copy(
            src_ref=prefix.at[NZ], dst_ref=x_total.at[x], send_sem=t_send.at[dx], recv_sem=t_recv.at[x],
            device_id=on_x(x + dx), device_id_type=MESH,
        )

    def from_x(xx):
        return pltpu.make_async_remote_copy(
            src_ref=prefix.at[NZ], dst_ref=x_total.at[xx], send_sem=t_send.at[0], recv_sem=t_recv.at[xx],
            device_id=on_x(xx), device_id_type=MESH,
        )

    def to_z(zz):
        return pltpu.make_async_remote_copy(
            src_ref=s_send.at[zz], dst_ref=s_in.at[mine], send_sem=s_send_sem.at[zz], recv_sem=s_recv.at[mine],
            device_id=on_z(zz), device_id_type=MESH,
        )

    @pl.when(is_owner)
    def _():
        prefix[0] = jnp.zeros((C, 2 * C), BF16)
        total = jnp.zeros((C, 2 * C), F32)
        for zz in range(NZ):
            @pl.when(z != zz)
            def _():
                from_z(zz).wait_recv()

            step = x_recv[zz]
            if zz == 0:
                total = step.astype(F32)
            else:
                total = total + nn(step[:, :C], total.astype(BF16)) + step.astype(F32)
            prefix[zz + 1] = total.astype(BF16)
        for dx in range(1, NX):
            @pl.when(x + dx < NX)
            def _():
                to_x(dx).start()

        state[...] = jnp.zeros_like(state)
        for xx in range(NX - 1):
            @pl.when(xx < x)
            def _():
                from_x(xx).wait_recv()
                step = x_total[xx]
                now = state[...]
                state[...] = now + nn(step[:, :C], now.astype(BF16)) + step[:, C:].astype(F32)

        start = state[...]
        start_b = start.astype(BF16)
        for zz in range(NZ):
            step = prefix[zz]
            here = (start + nn(step[:, :C], start_b) + step[:, C:].astype(F32)).astype(BF16)
            s_send[zz] = here

            @pl.when(z != zz)
            def _():
                to_z(zz).start()

            @pl.when(z == zz)
            def _():
                s_in[mine] = s_send[zz]

    wait_exchange(3)
    gain = gain_ref[...].astype(F32)

    def gates(c, carry):
        rows = block_rows(c)
        for n in range(HV):
            v = g_recv[rows, n * C : (n + 1) * C].astype(F32)
            gate[rows, n * C : (n + 1) * C] = v / (1.0 + jnp.exp(-v)) * gain
        return carry

    lax.fori_loop(0, NB, gates, 0)

    def to_sibling(n):
        cols = slice(n * C, (n + 1) * C)
        return pltpu.make_async_remote_copy(
            src_ref=g_mine.at[1 - core, :, cols], dst_ref=g_sib.at[:, cols],
            send_sem=sib_send.at[n], recv_sem=sib_recv.at[n],
            device_id=on_head(sibling), device_id_type=MESH,
        )

    for n in range(HV):
        @pl.when(z != 2 * n + core)
        def _():
            pltpu.make_async_remote_copy(
                src_ref=s_send.at[0], dst_ref=s_in.at[n], send_sem=s_send_sem.at[0], recv_sem=s_recv.at[n],
                device_id=on_z(2 * n + core), device_id_type=MESH,
            ).wait_recv()

        now = s_in[n]
        for c in range(NB):
            rows = slice(c * C, (c + 1) * C)
            values = nn(y_q[n, rows, :], now) + y_o[n, rows, :]
            spread = lax.rsqrt(jnp.mean(values * values, -1, keepdims=True) + EPS)
            gated = (values * spread * gate[rows, n * C : (n + 1) * C]).astype(BF16)
            for side in range(2):
                g_mine[side, c * ROWS : (c + 1) * ROWS, n * C : (n + 1) * C] = gated[
                    side * ROWS : (side + 1) * ROWS
                ]
        to_sibling(n).start()

    loads[5].wait()
    weight_copy.wait_recv()
    for n in range(HV):
        to_sibling(n).wait_recv()

    tile = 256

    def project(first):
        def one(t, carry):
            cols = pl.ds(pl.multiple_of(first + t * tile, tile), tile)
            value = nn(g_mine[core], w_own[:, cols]) + nn(g_sib[...], w_sib[:, cols])
            p_f[:, cols] = value
            p_b[:, cols] = value.astype(BF16)
            return carry

        lax.fori_loop(0, HALF // tile, one, 0)

    def rows_of(dy):
        return pl.ds(pl.multiple_of(lax.rem(y + dy, NY) * ROWS, ROWS), ROWS)

    a_cols, b_cols = slice(0, HALF), slice(HALF, DM)

    def ring(i, src, dst, dy):
        return pltpu.make_async_remote_copy(
            src_ref=src, dst_ref=dst, send_sem=rs_send.at[i], recv_sem=rs_recv.at[i],
            device_id=on_head(lax.rem(y + dy, NY) * 2 + core), device_id_type=MESH,
        )

    copies = [
        ring(0, p_b.at[rows_of(2), a_cols], relay_a, 1),
        ring(1, p_b.at[rows_of(3), a_cols], plus_a, 3),
        ring(2, p_b.at[rows_of(2), b_cols], relay_b, 3),
        ring(3, p_b.at[rows_of(1), b_cols], minus_b, 1),
        ring(4, join_a, minus_a, 1),
        ring(5, join_b, plus_b, 3),
    ]
    project(0)
    copies[0].start()
    copies[1].start()
    project(HALF)
    copies[2].start()
    copies[3].start()
    copies[0].wait_recv()
    join_a[...] = (p_f[rows_of(1), a_cols] + relay_a[...].astype(F32)).astype(BF16)
    copies[4].start()
    copies[2].wait_recv()
    join_b[...] = (p_f[rows_of(3), b_cols] + relay_b[...].astype(F32)).astype(BF16)
    copies[5].start()
    copies[1].wait_recv()
    copies[3].wait_recv()
    copies[4].wait_recv()
    out_ref[:, a_cols] = (
        p_f[rows_of(0), a_cols] + minus_a[...].astype(F32) + plus_a[...].astype(F32)
    ).astype(BF16)
    copies[5].wait_recv()
    out_ref[:, b_cols] = (
        p_f[rows_of(0), b_cols] + minus_b[...].astype(F32) + plus_b[...].astype(F32)
    ).astype(BF16)

    for array in range(4):
        for i in range(len(peers)):
            peer_copy(array, i).wait_send()
    weight_copy.wait_send()
    for n in range(HV):
        to_sibling(n).wait_send()

        @pl.when(z != 2 * n + core)
        def _():
            to_owner(n).wait_send()

    @pl.when(is_owner)
    def _():
        for dx in range(1, NX):
            @pl.when(x + dx < NX)
            def _():
                to_x(dx).wait_send()

        for zz in range(NZ):
            @pl.when(z != zz)
            def _():
                to_z(zz).wait_send()

    for copy in copies:
        copy.wait_send()


def per_device(queries, key_vectors, value_vectors, output_gate, write_strength, norm_gain, output_weight):
    any_space = pl.BlockSpec(memory_space=pl.ANY)
    vmem = pl.BlockSpec(memory_space=pltpu.VMEM)
    dma = pltpu.SemaphoreType.DMA
    v = pltpu.VMEM
    kh, vh = HK * NH, HV * NH
    scratch = [
        v((ROWS * kh, C), BF16), v((ROWS * kh, C), BF16), v((ROWS * vh, C), BF16), v((ROWS * vh, C), BF16),
        v((ROWS, vh), BF16), v((HV * C, DM), BF16), v((HV * C, DM), BF16),
        v((ROWS * kh, C), F32), v((ROWS * kh, C), F32), v((ROWS * vh, C), F32), v((ROWS * vh, C), F32),
        v((NH, ROWS, HK * C), BF16), v((NH, ROWS, HK * C + C), BF16), v((NH, ROWS, HV * C), BF16), v((NH, ROWS, HV * C), BF16),
        v((TOK, HK * C), BF16), v((TOK, HK * C + C), BF16), v((TOK, HV * C), BF16), v((TOK, HV * C), BF16),
        v((len(LEVELS), C, C), BF16), v((HK, NB, 8, C), F32), v((HK, NB, C, C), F32),
        v((HV, NB, C, C), BF16), v((HV, NB, C, C), BF16), v((HV, NB, C, 2 * C), BF16),
        v((HV, C, 2 * C), F32), v((HV, NB, C, 2 * C), BF16),
        v((HV, TOK, C), BF16), v((HV, TOK, C), F32), v((TOK, HV * C), F32),
        v((HV, C, 2 * C), BF16), v((NZ, C, 2 * C), BF16), v((NZ + 1, C, 2 * C), BF16), v((NX, C, 2 * C), BF16),
        v((C, C), F32), v((NZ, C, C), BF16), v((HV, C, C), BF16),
        v((2, NY * ROWS, HV * C), BF16), v((NY * ROWS, HV * C), BF16),
        v((NY * ROWS, DM), F32), v((NY * ROWS, DM), BF16),
        v((ROWS, HALF), BF16), v((ROWS, HALF), BF16), v((ROWS, HALF), BF16), v((ROWS, HALF), BF16),
        v((ROWS, HALF), BF16), v((ROWS, HALF), BF16), v((ROWS, HALF), BF16), v((ROWS, HALF), BF16),
        dma((6,)), dma((4,)), dma((4, 7)), dma((4, 7)), dma, dma,
        dma((HV,)), dma((NZ,)), dma((NX,)), dma((NX,)), dma((NZ,)), dma((HV,)),
        dma((HV,)), dma((HV,)), dma((6,)), dma((6,)),
    ]
    return pl.pallas_call(
        kernel,
        out_shape=jax.ShapeDtypeStruct((ROWS, DM), BF16),
        in_specs=[any_space] * 5 + [vmem, any_space],
        out_specs=vmem,
        scratch_shapes=scratch,
        compiler_params=pltpu.CompilerParams(
            collective_id=0, has_side_effects=True, vmem_limit_bytes=52 * 1024 * 1024
        ),
    )(
        queries.reshape(ROWS * kh, C),
        key_vectors.reshape(ROWS * kh, C),
        value_vectors.reshape(ROWS * vh, C),
        output_gate.reshape(ROWS * vh, C),
        write_strength,
        norm_gain.reshape(1, C),
        output_weight,
    )


def solution(mesh):
    placed = (
        P(("seq", "head"), None, None),
        P(("seq", "head"), None, None),
        P(("seq", "head"), None, None),
        P(("seq", "head"), None, None),
        P(("seq", "head"), None),
        P(),
        P("head", None),
    )
    return jax.shard_map(
        per_device, mesh=mesh, in_specs=placed, out_specs=P(("seq", "head"), None), check_vma=False
    )
```

time: 572 us -> 65.1 us (0.11)
  the two profiles are of different devices: /device:TPU:5 before, /device:TPU:23 now
where the time goes in v1:
time: 65.1 us; the launch traced here: 64.8 us
  Pallas kernels  58.7 us (90%)
  local copies, waits for them, and re-layouts  6.13 us (9%)
    pallas_call x1, Pallas kernels, per_device(): pl.pallas_call(kernel, out_shape=jax.ShapeDtypeStruct((ROWS, DM), BF16),...  58.7 us
    unnamed x12, local copies, waits for them, and re-layouts  6.13 us

profile of v1, /device:TPU:23, one launch (start us, length us, event | category | flops | bytes accessed | tf_op | source)
XLA Modules:
  0.0 64.8 jit_solution(10685304106934295527)
XLA Ops:
  0.0 0.8 %copy.8.b_hbm = bf16[64,32]{1,0:T(8,128)(2,1)S(1)} copy(bf16[64,32]{0,1:T(8,128)(2,1)} %param.11) | data formatting | bytes 8192 | tf_op args[4]
  0.8 0.0 copy-start
  0.8 1.0 %copy-done = bf16[64,32,128]{2,1,0:T(8,128)(2,1)S(1)} copy-done((bf16[64,32,128]{2,1,0:T(8,128)(2,1)S(1)}, bf16[64,32,128]{2,1,0:T(8,128)(2,1)}, u32[]{:S(2)}) %copy-start) | copy-done | bytes 524312
  1.8 0.0 copy-start.1
  1.8 1.0 %copy-done.1 = bf16[64,32,128]{2,1,0:T(8,128)(2,1)S(1)} copy-done((bf16[64,32,128]{2,1,0:T(8,128)(2,1)S(1)}, bf16[64,32,128]{2,1,0:T(8,128)(2,1)}, u32[]{:S(2)}) %copy-start.1) | copy-done | bytes 524312
  2.9 0.0 copy-start.2
  2.9 0.9 %copy-done.2 = bf16[64,16,128]{2,1,0:T(8,128)(2,1)S(1)} copy-done((bf16[64,16,128]{2,1,0:T(8,128)(2,1)S(1)}, bf16[64,16,128]{2,1,0:T(8,128)(2,1)}, u32[]{:S(2)}) %copy-start.2) | copy-done | bytes 262168
  3.8 0.0 copy-start.3
  3.8 0.9 %copy-done.3 = bf16[64,16,128]{2,1,0:T(8,128)(2,1)S(1)} copy-done((bf16[64,16,128]{2,1,0:T(8,128)(2,1)S(1)}, bf16[64,16,128]{2,1,0:T(8,128)(2,1)}, u32[]{:S(2)}) %copy-start.3) | copy-done | bytes 262168
  4.8 0.0 copy-start.4
  4.8 0.7 %copy-done.4 = bf16[128]{0:T(256)(128)(2,1)S(1)} copy-done((bf16[128]{0:T(256)(128)(2,1)S(1)}, bf16[128]{0:T(256)(128)(2,1)}, u32[]{:S(2)}) %copy-start.4) | copy-done | bytes 280
  5.4 58.7 %shard_map.73 = bf16[64,2048]{1,0:T(8,128)(2,1)S(1)} custom-call(bf16[1024,128]{1,0:T(8,128)(2,1)S(1)} %bitcast.7, bf16[1024,128]{1,0:T(8,128)(2,1)S(1)} %bitcast.8, bf16[2048,128]{1,0:T(8,128)(2,1)S(1)} %bitcast.5, bf16[2048,128]{1,0:T(8,128)(2,1)S(1)} %bitcast.6, bf16[64,32]{1,0:T(8,128)(2,1)S(1)} %copy.8.b_hbm, bf16[1,128]{1,0:T(2,128)(2,1)S(1)} %bitcast.9, ...), custom_call_target="tpu_custom_call" | custom-call | tf_op jit(solution)/shard_map/pallas_call | solution.py:490
  64.1 0.7 %copy.10 = bf16[64,2048]{1,0:T(8,128)(2,1)} copy(bf16[64,2048]{1,0:T(8,128)(2,1)S(1)} %shard_map.73) | data formatting | bytes 524288
Async XLA Ops:
  0.8 1.0 %copy-start = (bf16[64,32,128]{2,1,0:T(8,128)(2,1)S(1)}, bf16[64,32,128]{2,1,0:T(8,128)(2,1)}, u32[]{:S(2)}) copy-start(bf16[64,32,128]{2,1,0:T(8,128)(2,1)} %param.9) | copy-start | bytes 1572868
  1.8 1.0 %copy-start.1 = (bf16[64,32,128]{2,1,0:T(8,128)(2,1)S(1)}, bf16[64,32,128]{2,1,0:T(8,128)(2,1)}, u32[]{:S(2)}) copy-start(bf16[64,32,128]{2,1,0:T(8,128)(2,1)} %param.10) | copy-start | bytes 1572868
  2.9 0.9 %copy-start.2 = (bf16[64,16,128]{2,1,0:T(8,128)(2,1)S(1)}, bf16[64,16,128]{2,1,0:T(8,128)(2,1)}, u32[]{:S(2)}) copy-start(bf16[64,16,128]{2,1,0:T(8,128)(2,1)} %param.7) | copy-start | bytes 786436
  3.8 0.9 %copy-start.3 = (bf16[64,16,128]{2,1,0:T(8,128)(2,1)S(1)}, bf16[64,16,128]{2,1,0:T(8,128)(2,1)}, u32[]{:S(2)}) copy-start(bf16[64,16,128]{2,1,0:T(8,128)(2,1)} %param.8) | copy-start | bytes 786436
  4.8 0.7 %copy-start.4 = (bf16[128]{0:T(256)(128)(2,1)S(1)}, bf16[128]{0:T(256)(128)(2,1)}, u32[]{:S(2)}) copy-start(bf16[128]{0:T(256)(128)(2,1)} %param.12) | copy-start | bytes 772

commit v2 on v1

v2 whole, which is shorter than its diff:
```python
import functools

import jax
import jax.numpy as jnp
from jax import lax
from jax.experimental import pallas as pl
from jax.experimental.pallas import tpu as pltpu
from jax.sharding import PartitionSpec as P

F32 = jnp.float32
BF16 = jnp.bfloat16
MESH = pl.DeviceIdType.MESH
EPS = 1e-06
C = 128
ROWS = 64
NH = 8
NZ = 8
NX = 4
NY = 4
HV = 4
HK = 2
TOK = ROWS * NH
NB = TOK // C
DM = 2048
HALF = DM // 2
LEVELS = (2, 4, 8, 16, 32, 64)
KROWS = ROWS + 16


def nn(a, b):
    return jnp.dot(a, b, preferred_element_type=F32)


def nt(a, b):
    return lax.dot_general(a, b, (((1,), (1,)), ((), ())), preferred_element_type=F32)


def tn(a, b):
    return lax.dot_general(a, b, (((0,), (0,)), ((), ())), preferred_element_type=F32)


def block_rows(c):
    return pl.ds(pl.multiple_of(c * C, C), C)


def lower_rows(m, s):
    return jnp.concatenate([m[a + s : a + 2 * s] for a in range(0, C, 2 * s)], 0)


def double(xs, offs, s):
    bs = [x.astype(BF16) for x in xs]
    if s < 16:
        rights = [nn(o, b).astype(BF16) for o, b in zip(offs, bs)]
        return [x - nn(b, r) for x, b, r in zip(xs, bs, rights)]
    rights = [nn(lower_rows(o, s), b).astype(BF16) for o, b in zip(offs, bs)]
    zero = jnp.zeros((s, C), BF16)
    count = C // (2 * s)
    fulls = [
        jnp.concatenate(sum([[zero, r[i * s : (i + 1) * s]] for i in range(count)], []), 0) for r in rights
    ]
    steps = [nn(lower_rows(b, s), f) for b, f in zip(bs, fulls)]
    return [
        jnp.concatenate(
            sum(
                [
                    [x[2 * i * s : (2 * i + 1) * s], x[(2 * i + 1) * s : (2 * i + 2) * s] - d[i * s : (i + 1) * s]]
                    for i in range(count)
                ],
                [],
            ),
            0,
        )
        for x, d in zip(xs, steps)
    ]


def kernel(
    q_hbm, k_hbm, v_hbm, g_hbm, b_hbm, gain_ref, w_hbm, out_ref,
    q_in, k_in, v_in, g_in, b_in, w_own, w_sib,
    q_f, k_f, v_f, g_f, b_f,
    q_send, k_send, v_send, g_send,
    q_recv, k_recv, v_recv, g_recv,
    masks, rk_row, rk_col, x_u, moves, wu, ku, before,
    y_q, y_o, gate,
    t_mine, l_mine, t_all, l_all, t_join, t_pre, l_pre, t_row, l_row, state, s_send, s_in,
    g_mine, g_sib, p_f, p_b, relay_a, relay_b, join_a, join_b,
    minus_a, minus_b, plus_a, plus_b,
    in_sem, own_sem, a2a_send, a2a_recv, w_send_sem, w_recv_sem,
    t_send, t_recv, l_send, l_recv, tr_send, tr_recv, lr_send, lr_recv, s_send_sem, s_recv,
    sib_send, sib_recv, rs_send, rs_recv,
):
    seq = lax.axis_index("seq")
    head = lax.axis_index("head")
    x = seq // NZ
    z = lax.rem(seq, NZ)
    y = head // 2
    core = lax.rem(head, 2)
    sibling = y * 2 + (1 - core)

    def on_head(h):
        return (seq, h)

    def on_z(zz):
        return (x * NZ + zz, head)

    def on_x(xx):
        return (xx * NZ + z, head)

    peers = [(0, 1), (3, 0), (3, 1), (1, 0), (1, 1), (2, 0), (2, 1)]

    def head_at(dy, dc):
        return lax.rem(y + dy, NY) * 2 + lax.rem(core + dc, 2)

    barrier = pltpu.get_barrier_semaphore()
    for dy, dc in peers:
        pl.semaphore_signal(barrier, inc=1, device_id=on_head(head_at(dy, dc)), device_id_type=MESH)
    for dz in range(1, NZ):
        pl.semaphore_signal(barrier, inc=1, device_id=on_z(lax.rem(z + dz, NZ)), device_id_type=MESH)
    for dx in range(1, NX):
        pl.semaphore_signal(barrier, inc=1, device_id=on_x(lax.rem(x + dx, NX)), device_id_type=MESH)

    loads = [
        pltpu.make_async_copy(src, dst, in_sem.at[i])
        for i, (src, dst) in enumerate(
            [(k_hbm, k_in), (b_hbm, b_in), (v_hbm, v_in), (q_hbm, q_in), (g_hbm, g_in), (w_hbm, w_own)]
        )
    ]
    for copy in loads:
        copy.start()

    ri = lax.broadcasted_iota(jnp.int32, (C, C), 0)
    ci = lax.broadcasted_iota(jnp.int32, (C, C), 1)
    for i, s in enumerate(LEVELS):
        keep = (ri // (2 * s) == ci // (2 * s)) & (ri // s != ci // s)
        masks[i] = jnp.where(keep, 1.0, 0.0).astype(BF16)

    def to_columns(raw, wide, send, heads):
        per = heads // NH
        wide[...] = raw[...].astype(F32)
        for h in range(heads):
            send[h // per, :ROWS, (h % per) * C : (h % per + 1) * C] = wide[
                pl.ds(h, ROWS, stride=heads), :
            ].astype(BF16)

    sends = [(k_send, k_recv), (v_send, v_recv), (q_send, q_recv), (g_send, g_recv)]

    def peer_copy(array, i):
        send, recv = sends[array]
        target = head_at(*peers[i])
        return pltpu.make_async_remote_copy(
            src_ref=send.at[target],
            dst_ref=recv.at[head],
            send_sem=a2a_send.at[array, i],
            recv_sem=a2a_recv.at[array, i],
            device_id=on_head(target),
            device_id_type=MESH,
        )

    def own_copy(array):
        send, recv = sends[array]
        return pltpu.make_async_copy(send.at[head], recv.at[head], own_sem.at[array])

    def start_exchange(array):
        for i in range(len(peers)):
            peer_copy(array, i).start()
        own_copy(array).start()

    def wait_exchange(array):
        own_copy(array).wait()
        for i in range(len(peers)):
            peer_copy(array, i).wait_recv()

    def block(recv, c, cols):
        return jnp.concatenate([recv[2 * c + i, :ROWS, cols] for i in range(2)], 0)

    loads[0].wait()
    loads[1].wait()
    to_columns(k_in, k_f, k_send, HK * NH)
    lanes = lax.broadcasted_iota(jnp.int32, (ROWS, C), 1) - ROWS * lax.rem(head, 2)
    place = jnp.where(lanes == lax.broadcasted_iota(jnp.int32, (ROWS, C), 0), 1.0, 0.0).astype(BF16)
    b_f[: HV * NH, :] = nn(b_in[...], place)
    b_f[HV * NH :, :] = jnp.zeros((16, C), F32)
    for h in range(NH):
        k_send[h, ROWS:, :C] = b_f[h * HV : h * HV + 16, :].astype(BF16)
        k_send[h, ROWS:, C:] = jnp.zeros((16, C), BF16)
    pl.semaphore_wait(barrier, len(peers) + (NZ - 1) + (NX - 1))
    start_exchange(0)
    loads[2].wait()
    to_columns(v_in, v_f, v_send, HV * NH)
    start_exchange(1)
    loads[3].wait()
    to_columns(q_in, q_f, q_send, HK * NH)
    start_exchange(2)
    loads[4].wait()
    to_columns(g_in, g_f, g_send, HV * NH)
    start_exchange(3)
    weight_copy = pltpu.make_async_remote_copy(
        src_ref=w_hbm, dst_ref=w_sib, send_sem=w_send_sem, recv_sem=w_recv_sem,
        device_id=on_head(sibling), device_id_type=MESH,
    )
    weight_copy.start()

    eye = ri == ci

    def invert(blocks):
        todo = []
        for c in blocks:
            sums = sum(k_recv[2 * c + i, ROWS:, :C].astype(F32) for i in range(2))
            for j in range(HK):
                kb = block(k_recv, c, slice(j * C, (j + 1) * C))
                gram = nt(kb, kb)
                diag = jnp.where(eye, gram, 0.0)
                kc = lax.rsqrt(jnp.sum(diag, 1, keepdims=True) + EPS)
                kr = lax.rsqrt(jnp.sum(diag, 0, keepdims=True) + EPS)
                rk_row[j, c] = jnp.broadcast_to(kr, (8, C))
                rk_col[j, c] = jnp.broadcast_to(kc, (C, C))
                scaled = jnp.where(ri > ci, gram * kc * kr, 0.0)
                for n in (2 * j, 2 * j + 1):
                    br = sums[n : n + 1]
                    bc = jnp.sum(jnp.where(eye, br, 0.0), 1, keepdims=True)
                    a = scaled * bc
                    first = jnp.where(eye, 1.0, jnp.where(ri // 2 == ci // 2, -a, 0.0))
                    todo.append((n, c, a.astype(BF16), br, kr, kc, kb, first))
        xs = [t[-1] for t in todo]
        for i, s in enumerate(LEVELS):
            xs = double(xs, [t[2] * masks[i] for t in todo], s)
        ws = []
        for (n, c, _, br, kr, kc, kb, _), x in zip(todo, xs):
            right = x * br
            x_u[n, c] = right.astype(BF16)
            ws.append(nn((right * kr).astype(BF16), kb))
        for (n, c, _, br, kr, kc, kb, _), w in zip(todo, ws):
            wu[n, c, :, :C] = w.astype(BF16)
            moves[n, c] = tn(kb, (w * -kc).astype(BF16))

    def wait_keys(some):
        for i in some:
            peer_copy(0, i).wait_recv()

    own_copy(0).wait()
    wait_keys((0, 1, 2))
    invert((y, lax.rem(y + 1, NY)))
    wait_keys((3, 4, 5, 6))
    invert((lax.rem(y + 3, NY), lax.rem(y + 2, NY)))

    is_owner = lax.rem(z, 2) == core
    mine = z // 2

    def to_owner(mine_ref, all_ref, send, recv, n):
        return pltpu.make_async_remote_copy(
            src_ref=mine_ref.at[n], dst_ref=all_ref.at[z], send_sem=send.at[n], recv_sem=recv.at[z],
            device_id=on_z(2 * n + core), device_id_type=MESH,
        )

    def from_z(mine_ref, all_ref, send, recv, zz):
        return pltpu.make_async_remote_copy(
            src_ref=mine_ref.at[0], dst_ref=all_ref.at[zz], send_sem=send.at[0], recv_sem=recv.at[zz],
            device_id=on_z(zz), device_id_type=MESH,
        )

    t_refs = (t_mine, t_all, t_send, t_recv)
    l_refs = (l_mine, l_all, l_send, l_recv)

    def hand_in(refs):
        for n in range(HV):
            @pl.when(z != 2 * n + core)
            def _():
                to_owner(*refs, n).start()

            @pl.when(z == 2 * n + core)
            def _():
                refs[1][z] = refs[0][n]

    def gather(refs):
        for zz in range(NZ):
            @pl.when(z != zz)
            def _():
                from_z(*refs, zz).wait_recv()

    ts = [moves[n, 0] for n in range(HV)]
    for n in range(HV):
        before[n, 0] = jnp.zeros((C, 2 * C), BF16)
    for c in range(1, NB):
        tb = [t.astype(BF16) for t in ts]
        for n in range(HV):
            before[n, c, :, :C] = tb[n]
        step = [moves[n, c] for n in range(HV)]
        ts = [t + nn(m.astype(BF16), b) + m for t, m, b in zip(ts, step, tb)]
    for n in range(HV):
        t_mine[n] = ts[n].astype(BF16)
    hand_in(t_refs)

    wait_exchange(1)
    pair = 2

    def values(step, carry):
        todo = [(n, step * pair + i) for i in range(pair) for n in range(HV)]
        us = [nn(x_u[n, c], block(v_recv, c, slice(n * C, (n + 1) * C))) for n, c in todo]
        for (n, c), u in zip(todo, us):
            wu[n, c, :, C:] = u.astype(BF16)
        for (n, c), u in zip(todo, us):
            j = n // 2
            kb = block(k_recv, c, slice(j * C, (j + 1) * C))
            ku[n, c] = tn(kb, (u * rk_col[j, c]).astype(BF16))
        return carry

    lax.fori_loop(0, NB // pair, values, 0)
    ls = [ku[n, 0] for n in range(HV)]
    for c in range(1, NB):
        lb = [l.astype(BF16) for l in ls]
        for n in range(HV):
            before[n, c, :, C:] = lb[n]
        ls = [ls[n] + nn(moves[n, c].astype(BF16), lb[n]) + ku[n, c] for n in range(HV)]
    for n in range(HV):
        l_mine[n] = ls[n].astype(BF16)
    hand_in(l_refs)

    wait_exchange(2)

    def outputs(c, carry):
        rows = block_rows(c)
        for j in range(HK):
            qb = block(q_recv, c, slice(j * C, (j + 1) * C))
            kb = block(k_recv, c, slice(j * C, (j + 1) * C))
            qf = qb.astype(F32)
            qc = lax.rsqrt(jnp.sum(qf * qf, 1, keepdims=True) + EPS) * (C ** -0.5)
            scores = jnp.where(ri >= ci, nt(qb, kb) * qc * rk_row[j, c, 0:1, :], 0.0).astype(BF16)
            unit = qf * qc
            for n in (2 * j, 2 * j + 1):
                part = nn(scores, wu[n, c])
                eff = unit - part[:, :C]
                moved = nn(eff.astype(BF16), before[n, c])
                y_q[n, rows, :] = (eff + moved[:, :C]).astype(BF16)
                y_o[n, rows, :] = part[:, C:] + moved[:, C:]
        return carry

    lax.fori_loop(0, NB, outputs, 0)

    wait_exchange(3)
    gain = gain_ref[...].astype(F32)

    def gates(c, carry):
        rows = block_rows(c)
        for n in range(HV):
            v = block(g_recv, c, slice(n * C, (n + 1) * C)).astype(F32)
            gate[rows, n * C : (n + 1) * C] = v / (1.0 + jnp.exp(-v)) * gain
        return carry

    lax.fori_loop(0, NB, gates, 0)

    tree = [
        [((1,), 0), ((3,), 2), ((5,), 4), ((7,), 6)],
        [((2, 3), 1), ((6, 7), 5)],
        [((4, 5, 6, 7), 3)],
    ]

    def to_x(row, send, recv, dx):
        return pltpu.make_async_remote_copy(
            src_ref=row.at[x], dst_ref=row.at[x], send_sem=send.at[dx], recv_sem=recv.at[x],
            device_id=on_x(x + dx), device_id_type=MESH,
        )

    def from_x(row, send, recv, xx):
        return pltpu.make_async_remote_copy(
            src_ref=row.at[xx], dst_ref=row.at[xx], send_sem=send.at[0], recv_sem=recv.at[xx],
            device_id=on_x(xx), device_id_type=MESH,
        )

    t_line = (t_row, tr_send, tr_recv)
    l_line = (l_row, lr_send, lr_recv)

    def to_z(zz):
        return pltpu.make_async_remote_copy(
            src_ref=s_send.at[zz], dst_ref=s_in.at[mine], send_sem=s_send_sem.at[zz], recv_sem=s_recv.at[mine],
            device_id=on_z(zz), device_id_type=MESH,
        )

    @pl.when(is_owner)
    def _():
        gather(t_refs)
        now = [t_all[zz] for zz in range(NZ)]
        for i, level in enumerate(tree):
            news = {}
            m = 0
            for laters, earlier in level:
                left = jnp.concatenate([now[later] for later in laters], 0)
                t_join[i, m * C : (m + len(laters)) * C] = left
                moved = nn(left, now[earlier])
                for a, later in enumerate(laters):
                    both = now[later].astype(F32) + now[earlier].astype(F32)
                    news[later] = (both + moved[a * C : (a + 1) * C]).astype(BF16)
                m += len(laters)
            for later in news:
                now[later] = news[later]
        for zz in range(NZ):
            t_pre[zz] = now[zz]
        t_row[x] = now[NZ - 1]
        for dx in range(1, NX):
            @pl.when((x > 0) & (x + dx < NX))
            def _():
                to_x(*t_line, dx).start()

        gather(l_refs)
        for zz in range(NZ):
            l_pre[zz] = l_all[zz].astype(F32)
        for i, level in enumerate(tree):
            m = 0
            for laters, earlier in level:
                first = l_pre[earlier]
                moved = nn(t_join[i, m * C : (m + len(laters)) * C], first.astype(BF16))
                for a, later in enumerate(laters):
                    l_pre[later] = l_pre[later] + first + moved[a * C : (a + 1) * C]
                m += len(laters)
        l_row[x] = l_pre[NZ - 1].astype(BF16)
        for dx in range(1, NX):
            @pl.when(x + dx < NX)
            def _():
                to_x(*l_line, dx).start()

        state[...] = jnp.zeros_like(state)
        for xx in range(NX - 1):
            @pl.when(xx < x)
            def _():
                from_x(*l_line, xx).wait_recv()
                row = l_row[xx].astype(F32)
                if xx == 0:
                    state[...] = row
                else:
                    from_x(*t_line, xx).wait_recv()
                    held = state[...]
                    state[...] = held + nn(t_row[xx], held.astype(BF16)) + row

        start = state[...]
        start_b = start.astype(BF16)
        for zz in range(NZ):
            if zz == 0:
                s_send[zz] = start_b
            else:
                s_send[zz] = (start + nn(t_pre[zz - 1], start_b) + l_pre[zz - 1]).astype(BF16)

            @pl.when(z != zz)
            def _():
                to_z(zz).start()

            @pl.when(z == zz)
            def _():
                s_in[mine] = s_send[zz]

    def to_sibling(n):
        cols = slice(n * C, (n + 1) * C)
        return pltpu.make_async_remote_copy(
            src_ref=g_mine.at[1 - core, :, cols], dst_ref=g_sib.at[:, cols],
            send_sem=sib_send.at[n], recv_sem=sib_recv.at[n],
            device_id=on_head(sibling), device_id_type=MESH,
        )

    for n in range(HV):
        @pl.when(z != 2 * n + core)
        def _():
            pltpu.make_async_remote_copy(
                src_ref=s_send.at[0], dst_ref=s_in.at[n], send_sem=s_send_sem.at[0], recv_sem=s_recv.at[n],
                device_id=on_z(2 * n + core), device_id_type=MESH,
            ).wait_recv()

        now = s_in[n]
        for c in range(NB):
            rows = slice(c * C, (c + 1) * C)
            values = nn(y_q[n, rows, :], now) + y_o[n, rows, :]
            spread = lax.rsqrt(jnp.mean(values * values, -1, keepdims=True) + EPS)
            gated = (values * spread * gate[rows, n * C : (n + 1) * C]).astype(BF16)
            for side in range(2):
                g_mine[side, c * ROWS : (c + 1) * ROWS, n * C : (n + 1) * C] = gated[
                    side * ROWS : (side + 1) * ROWS
                ]
        to_sibling(n).start()

    loads[5].wait()
    weight_copy.wait_recv()
    for n in range(HV):
        to_sibling(n).wait_recv()

    tile, piece = 256, 512

    def project(first):
        def one(t, carry):
            cols = pl.ds(pl.multiple_of(first + t * tile, tile), tile)
            value = nn(g_mine[core], w_own[:, cols]) + nn(g_sib[...], w_sib[:, cols])
            p_f[:, cols] = value
            p_b[:, cols] = value.astype(BF16)
            return carry

        lax.fori_loop(0, piece // tile, one, 0)

    def rows_of(dy):
        return pl.ds(pl.multiple_of(lax.rem(y + dy, NY) * ROWS, ROWS), ROWS)

    def ring(i, src, dst, dy):
        return pltpu.make_async_remote_copy(
            src_ref=src, dst_ref=dst, send_sem=rs_send.at[i], recv_sem=rs_recv.at[i],
            device_id=on_head(lax.rem(y + dy, NY) * 2 + core), device_id_type=MESH,
        )

    a_cols, b_cols = slice(0, HALF), slice(HALF, DM)
    near = [slice(0, piece), slice(piece, HALF)]
    far = [slice(HALF, HALF + piece), slice(HALF + piece, DM)]
    relays_a = [ring(i, p_b.at[rows_of(2), near[i]], relay_a.at[:, near[i]], 1) for i in range(2)]
    relays_b = [ring(2 + i, p_b.at[rows_of(2), far[i]], relay_b.at[:, near[i]], 3) for i in range(2)]
    alone_a = ring(4, p_b.at[rows_of(3), a_cols], plus_a, 3)
    alone_b = ring(5, p_b.at[rows_of(1), b_cols], minus_b, 1)
    joins_a = [ring(6 + i, join_a.at[:, near[i]], minus_a.at[:, near[i]], 1) for i in range(2)]
    joins_b = [ring(8 + i, join_b.at[:, near[i]], plus_b.at[:, near[i]], 3) for i in range(2)]
    copies = relays_a + relays_b + [alone_a, alone_b] + joins_a + joins_b
    for i in range(2):
        project(i * piece)
        relays_a[i].start()
        project(HALF + i * piece)
        relays_b[i].start()
    alone_a.start()
    alone_b.start()
    for i in range(2):
        relays_a[i].wait_recv()
        join_a[:, near[i]] = (p_f[rows_of(1), near[i]] + relay_a[:, near[i]].astype(F32)).astype(BF16)
        joins_a[i].start()
        relays_b[i].wait_recv()
        join_b[:, near[i]] = (p_f[rows_of(3), far[i]] + relay_b[:, near[i]].astype(F32)).astype(BF16)
        joins_b[i].start()
    alone_a.wait_recv()
    alone_b.wait_recv()
    for i in range(2):
        joins_a[i].wait_recv()
        out_ref[:, near[i]] = (
            p_f[rows_of(0), near[i]] + minus_a[:, near[i]].astype(F32) + plus_a[:, near[i]].astype(F32)
        ).astype(BF16)
        joins_b[i].wait_recv()
        out_ref[:, far[i]] = (
            p_f[rows_of(0), far[i]] + minus_b[:, near[i]].astype(F32) + plus_b[:, near[i]].astype(F32)
        ).astype(BF16)

    for array in range(4):
        for i in range(len(peers)):
            peer_copy(array, i).wait_send()
    weight_copy.wait_send()
    for n in range(HV):
        to_sibling(n).wait_send()

        @pl.when(z != 2 * n + core)
        def _():
            to_owner(*t_refs, n).wait_send()
            to_owner(*l_refs, n).wait_send()

    @pl.when(is_owner)
    def _():
        for dx in range(1, NX):
            @pl.when((x > 0) & (x + dx < NX))
            def _():
                to_x(*t_line, dx).wait_send()

            @pl.when(x + dx < NX)
            def _():
                to_x(*l_line, dx).wait_send()

        for zz in range(NZ):
            @pl.when(z != zz)
            def _():
                to_z(zz).wait_send()

    for copy in copies:
        copy.wait_send()


def per_device(queries, key_vectors, value_vectors, output_gate, write_strength, norm_gain, output_weight):
    any_space = pl.BlockSpec(memory_space=pl.ANY)
    vmem = pl.BlockSpec(memory_space=pltpu.VMEM)
    dma = pltpu.SemaphoreType.DMA
    v = pltpu.VMEM
    kh, vh = HK * NH, HV * NH
    half = v((ROWS, HALF), BF16)
    scratch = [
        v((ROWS * kh, C), BF16), v((ROWS * kh, C), BF16), v((ROWS * vh, C), BF16), v((ROWS * vh, C), BF16),
        v((vh, ROWS), BF16), v((HV * C, DM), BF16), v((HV * C, DM), BF16),
        v((ROWS * kh, C), F32), v((ROWS * kh, C), F32), v((ROWS * vh, C), F32), v((ROWS * vh, C), F32), v((vh + 16, C), F32),
        v((NH, ROWS, HK * C), BF16), v((NH, KROWS, HK * C), BF16), v((NH, ROWS, HV * C), BF16), v((NH, ROWS, HV * C), BF16),
        v((NH, ROWS, HK * C), BF16), v((NH, KROWS, HK * C), BF16), v((NH, ROWS, HV * C), BF16), v((NH, ROWS, HV * C), BF16),
        v((len(LEVELS), C, C), BF16), v((HK, NB, 8, C), F32), v((HK, NB, C, C), F32),
        v((HV, NB, C, C), BF16), v((HV, NB, C, C), F32), v((HV, NB, C, 2 * C), BF16), v((HV, NB, C, C), F32),
        v((HV, NB, C, 2 * C), BF16),
        v((HV, TOK, C), BF16), v((HV, TOK, C), F32), v((TOK, HV * C), F32),
        v((HV, C, C), BF16), v((HV, C, C), BF16), v((NZ, C, C), BF16), v((NZ, C, C), BF16),
        v((3, 4 * C, C), BF16), v((NZ, C, C), BF16), v((NZ, C, C), F32), v((NX, C, C), BF16), v((NX, C, C), BF16),
        v((C, C), F32), v((NZ, C, C), BF16), v((HV, C, C), BF16),
        v((2, NY * ROWS, HV * C), BF16), v((NY * ROWS, HV * C), BF16),
        v((NY * ROWS, DM), F32), v((NY * ROWS, DM), BF16),
        half, half, half, half, half, half, half, half,
        dma((6,)), dma((4,)), dma((4, 7)), dma((4, 7)), dma, dma,
        dma((HV,)), dma((NZ,)), dma((HV,)), dma((NZ,)), dma((NX,)), dma((NX,)), dma((NX,)), dma((NX,)),
        dma((NZ,)), dma((HV,)),
        dma((HV,)), dma((HV,)), dma((10,)), dma((10,)),
    ]
    return pl.pallas_call(
        kernel,
        out_shape=jax.ShapeDtypeStruct((ROWS, DM), BF16),
        in_specs=[any_space] * 5 + [vmem, any_space],
        out_specs=vmem,
        scratch_shapes=scratch,
        compiler_params=pltpu.CompilerParams(
            collective_id=0, has_side_effects=True, vmem_limit_bytes=60 * 1024 * 1024
        ),
    )(
        queries.reshape(ROWS * kh, C),
        key_vectors.reshape(ROWS * kh, C),
        value_vectors.reshape(ROWS * vh, C),
        output_gate.reshape(ROWS * vh, C),
        write_strength.T,
        norm_gain.reshape(1, C),
        output_weight,
    )


def solution(mesh):
    placed = (
        P(("seq", "head"), None, None),
        P(("seq", "head"), None, None),
        P(("seq", "head"), None, None),
        P(("seq", "head"), None, None),
        P(("seq", "head"), None),
        P(),
        P("head", None),
    )
    return jax.shard_map(
        per_device, mesh=mesh, in_specs=placed, out_specs=P(("seq", "head"), None), check_vma=False
    )
```

time: 65.1 us -> 54.5 us (0.84)
  the two profiles are of different devices: /device:TPU:23 before, /device:TPU:5 now
where the time goes in v2:
time: 54.5 us; the launch traced here: 54 us
  Pallas kernels  52.3 us (96%)
  local copies, waits for them, and re-layouts  1.67 us (3%)
    pallas_call x1, Pallas kernels, per_device(): pl.pallas_call(kernel, out_shape=jax.ShapeDtypeStruct((ROWS, DM), BF16),...  52.3 us
    unnamed x1, local copies, waits for them, and re-layouts  1.67 us

profile of v2, /device:TPU:5, one launch (start us, length us, event | category | flops | bytes accessed | tf_op | source)
XLA Modules:
  0.0 54.0 jit_solution(6957005793901787659)
XLA Ops:
  0.0 52.3 %shard_map.73 = bf16[64,2048]{1,0:T(8,128)(2,1)} custom-call(bf16[1024,128]{1,0:T(8,128)(2,1)} %bitcast.8, bf16[1024,128]{1,0:T(8,128)(2,1)} %bitcast.9, bf16[2048,128]{1,0:T(8,128)(2,1)} %bitcast.6, bf16[2048,128]{1,0:T(8,128)(2,1)} %bitcast.7, bf16[32,64]{1,0:T(8,128)(2,1)} %bitcast.10, bf16[1,128]{1,0:T(2,128)(2,1)} %bitcast.11, bf16[512,2048]{1,0:T(8,128)(2,1)} %w_hbm.1), custom_call_target="tpu_custom_call" | custom-call | tf_op jit(solution)/shard_map/pallas_call | solution.py:599
  52.3 1.7 %copy.9 = bf16[64,2048]{1,0:T(8,128)(2,1)} copy(bf16[64,2048]{1,0:T(8,128)(2,1)} %shard_map.73) | data formatting | bytes 524288

commit v3 on v2

--- a/solution.py
+++ b/solution.py
@@ -75,19 +75,19 @@
 
 
 def kernel(
-    q_hbm, k_hbm, v_hbm, g_hbm, b_hbm, gain_ref, w_hbm, out_ref,
+    q_hbm, k_hbm, v_hbm, g_hbm, b_hbm, gain_hbm, w_hbm, out_hbm,
     q_in, k_in, v_in, g_in, b_in, w_own, w_sib,
     q_f, k_f, v_f, g_f, b_f,
     q_send, k_send, v_send, g_send,
     q_recv, k_recv, v_recv, g_recv,
     masks, rk_row, rk_col, x_u, moves, wu, ku, before,
     y_q, y_o, gate,
-    t_mine, l_mine, t_all, l_all, t_join, t_pre, l_pre, t_row, l_row, state, s_send, s_in,
+    t_late, t_mine, l_mine, t_all, l_all, t_after, t_join, t_pre, l_pre, t_row, l_row, state, s_send, s_in,
     g_mine, g_sib, p_f, p_b, relay_a, relay_b, join_a, join_b,
     minus_a, minus_b, plus_a, plus_b,
     in_sem, own_sem, a2a_send, a2a_recv, w_send_sem, w_recv_sem,
     t_send, t_recv, l_send, l_recv, tr_send, tr_recv, lr_send, lr_recv, s_send_sem, s_recv,
-    sib_send, sib_recv, rs_send, rs_recv,
+    sib_send, sib_recv, rs_send, rs_recv, out_v, out_sem, gain_in,
 ):
     seq = lax.axis_index("seq")
     head = lax.axis_index("head")
@@ -122,7 +122,7 @@
     loads = [
         pltpu.make_async_copy(src, dst, in_sem.at[i])
         for i, (src, dst) in enumerate(
-            [(k_hbm, k_in), (b_hbm, b_in), (v_hbm, v_in), (q_hbm, q_in), (g_hbm, g_in), (w_hbm, w_own)]
+            [(k_hbm, k_in), (b_hbm, b_in), (v_hbm, v_in), (q_hbm, q_in), (g_hbm, g_in), (w_hbm, w_own), (gain_hbm, gain_in)]
         )
     ]
     for copy in loads:
@@ -187,18 +187,17 @@
     start_exchange(0)
     loads[2].wait()
     to_columns(v_in, v_f, v_send, HV * NH)
-    start_exchange(1)
     loads[3].wait()
     to_columns(q_in, q_f, q_send, HK * NH)
-    start_exchange(2)
     loads[4].wait()
     to_columns(g_in, g_f, g_send, HV * NH)
-    start_exchange(3)
+    for i in range(len(peers)):
+        peer_copy(0, i).wait_send()
+    start_exchange(1)
     weight_copy = pltpu.make_async_remote_copy(
         src_ref=w_hbm, dst_ref=w_sib, send_sem=w_send_sem, recv_sem=w_recv_sem,
         device_id=on_head(sibling), device_id_type=MESH,
     )
-    weight_copy.start()
 
     eye = ri == ci
 
@@ -238,10 +237,21 @@
             peer_copy(0, i).wait_recv()
 
     own_copy(0).wait()
-    wait_keys((0, 1, 2))
-    invert((y, lax.rem(y + 1, NY)))
-    wait_keys((3, 4, 5, 6))
-    invert((lax.rem(y + 3, NY), lax.rem(y + 2, NY)))
+    wait_keys((0,))
+
+    def halves(step, carry):
+        @pl.when(step == 0)
+        def _():
+            wait_keys((1, 2))
+
+        @pl.when(step == 1)
+        def _():
+            wait_keys((3, 4, 5, 6))
+
+        invert((lax.rem(y + 3 * step, NY), lax.rem(y + 1 + step, NY)))
+        return carry
+
+    lax.fori_loop(0, 2, halves, 0)
 
     is_owner = lax.rem(z, 2) == core
     mine = z // 2
@@ -277,20 +287,27 @@
             def _():
                 from_z(*refs, zz).wait_recv()
 
-    ts = [moves[n, 0] for n in range(HV)]
     for n in range(HV):
         before[n, 0] = jnp.zeros((C, 2 * C), BF16)
-    for c in range(1, NB):
-        tb = [t.astype(BF16) for t in ts]
-        for n in range(HV):
-            before[n, c, :, :C] = tb[n]
-        step = [moves[n, c] for n in range(HV)]
-        ts = [t + nn(m.astype(BF16), b) + m for t, m, b in zip(ts, step, tb)]
+    m_f = [[moves[n, c] for c in range(NB)] for n in range(HV)]
+    m_b = [[m.astype(BF16) for m in ms] for ms in m_f]
+    early = [(fs[0] + fs[1] + nn(bs[1], bs[0])).astype(BF16) for fs, bs in zip(m_f, m_b)]
+    late = [fs[2] + fs[3] + nn(bs[3], bs[2]) for fs, bs in zip(m_f, m_b)]
+    for n in range(HV):
+        t_late[n] = late[n].astype(BF16)
+    ts = [a.astype(F32) + b + nn(b.astype(BF16), a) for a, b in zip(early, late)]
     for n in range(HV):
         t_mine[n] = ts[n].astype(BF16)
     hand_in(t_refs)
+    for n in range(HV):
+        before[n, 1, :, :C] = m_b[n][0]
+        before[n, 2, :, :C] = early[n]
+        before[n, 3, :, :C] = (m_f[n][2] + early[n].astype(F32) + nn(m_b[n][2], early[n])).astype(BF16)
 
     wait_exchange(1)
+    start_exchange(2)
+    start_exchange(3)
+    weight_copy.start()
     pair = 2
 
     def values(step, carry):
@@ -305,49 +322,21 @@
         return carry
 
     lax.fori_loop(0, NB // pair, values, 0)
-    ls = [ku[n, 0] for n in range(HV)]
-    for c in range(1, NB):
-        lb = [l.astype(BF16) for l in ls]
-        for n in range(HV):
-            before[n, c, :, C:] = lb[n]
-        ls = [ls[n] + nn(moves[n, c].astype(BF16), lb[n]) + ku[n, c] for n in range(HV)]
+    first = [ku[n, 0].astype(BF16) for n in range(HV)]
+    third = [ku[n, 2].astype(BF16) for n in range(HV)]
+    early = [ku[n, 0] + ku[n, 1] + nn(moves[n, 1].astype(BF16), first[n]) for n in range(HV)]
+    late = [ku[n, 2] + ku[n, 3] + nn(moves[n, 3].astype(BF16), third[n]) for n in range(HV)]
+    early_b = [e.astype(BF16) for e in early]
+    ls = [early[n] + late[n] + nn(t_late[n], early_b[n]) for n in range(HV)]
     for n in range(HV):
         l_mine[n] = ls[n].astype(BF16)
     hand_in(l_refs)
-
-    wait_exchange(2)
-
-    def outputs(c, carry):
-        rows = block_rows(c)
-        for j in range(HK):
-            qb = block(q_recv, c, slice(j * C, (j + 1) * C))
-            kb = block(k_recv, c, slice(j * C, (j + 1) * C))
-            qf = qb.astype(F32)
-            qc = lax.rsqrt(jnp.sum(qf * qf, 1, keepdims=True) + EPS) * (C ** -0.5)
-            scores = jnp.where(ri >= ci, nt(qb, kb) * qc * rk_row[j, c, 0:1, :], 0.0).astype(BF16)
-            unit = qf * qc
-            for n in (2 * j, 2 * j + 1):
-                part = nn(scores, wu[n, c])
-                eff = unit - part[:, :C]
-                moved = nn(eff.astype(BF16), before[n, c])
-                y_q[n, rows, :] = (eff + moved[:, :C]).astype(BF16)
-                y_o[n, rows, :] = part[:, C:] + moved[:, C:]
-        return carry
-
-    lax.fori_loop(0, NB, outputs, 0)
-
-    wait_exchange(3)
-    gain = gain_ref[...].astype(F32)
-
-    def gates(c, carry):
-        rows = block_rows(c)
-        for n in range(HV):
-            v = block(g_recv, c, slice(n * C, (n + 1) * C)).astype(F32)
-            gate[rows, n * C : (n + 1) * C] = v / (1.0 + jnp.exp(-v)) * gain
-        return carry
-
-    lax.fori_loop(0, NB, gates, 0)
-
+    for n in range(HV):
+        before[n, 1, :, C:] = first[n]
+        before[n, 2, :, C:] = early_b[n]
+        before[n, 3, :, C:] = (ku[n, 2] + early[n] + nn(moves[n, 2].astype(BF16), early_b[n])).astype(BF16)
+
+    assert NB == 4 and NZ == 8 and NX == 4
     tree = [
         [((1,), 0), ((3,), 2), ((5,), 4), ((7,), 6)],
         [((2, 3), 1), ((6, 7), 5)],
@@ -394,6 +383,19 @@
                 now[later] = news[later]
         for zz in range(NZ):
             t_pre[zz] = now[zz]
+
+        def join(later, earlier):
+            return (later.astype(F32) + earlier.astype(F32) + nn(later, earlier)).astype(BF16)
+
+        all_t = [t_all[zz] for zz in range(NZ)]
+        p32, p54 = t_join[1, C : 2 * C], t_join[2, C : 2 * C]
+        p76, p74 = t_join[1, 3 * C :], t_join[2, 3 * C :]
+        p21 = join(p32, all_t[1])
+        for zz, value in [
+            (0, join(p74, p21)), (1, join(p74, p32)), (2, join(p74, all_t[3])), (3, p74),
+            (4, join(p76, all_t[5])), (5, p76), (6, all_t[7]),
+        ]:
+            t_after[:, zz * C : (zz + 1) * C] = value
         t_row[x] = now[NZ - 1]
         for dx in range(1, NX):
             @pl.when((x > 0) & (x + dx < NX))
@@ -401,8 +403,17 @@
                 to_x(*t_line, dx).start()
 
         gather(l_refs)
+        lead = l_all[: NZ - 1].reshape((NZ - 1) * C, C)
+        row = nn(t_after[...], lead)
         for zz in range(NZ):
             l_pre[zz] = l_all[zz].astype(F32)
+            row = row + l_pre[zz]
+        l_row[x] = row.astype(BF16)
+        for dx in range(1, NX):
+            @pl.when(x + dx < NX)
+            def _():
+                to_x(*l_line, dx).start()
+
         for i, level in enumerate(tree):
             m = 0
             for laters, earlier in level:
@@ -411,24 +422,34 @@
                 for a, later in enumerate(laters):
                     l_pre[later] = l_pre[later] + first + moved[a * C : (a + 1) * C]
                 m += len(laters)
-        l_row[x] = l_pre[NZ - 1].astype(BF16)
-        for dx in range(1, NX):
-            @pl.when(x + dx < NX)
-            def _():
-                to_x(*l_line, dx).start()
-
-        state[...] = jnp.zeros_like(state)
-        for xx in range(NX - 1):
-            @pl.when(xx < x)
-            def _():
+
+        @pl.when(x == 0)
+        def _():
+            state[...] = jnp.zeros_like(state)
+
+        @pl.when(x == 1)
+        def _():
+            from_x(*l_line, 0).wait_recv()
+            state[...] = l_row[0].astype(F32)
+
+        @pl.when(x == 2)
+        def _():
+            from_x(*t_line, 1).wait_recv()
+            from_x(*l_line, 0).wait_recv()
+            from_x(*l_line, 1).wait_recv()
+            state[...] = nn(t_row[1], l_row[0]) + l_row[0].astype(F32) + l_row[1].astype(F32)
+
+        @pl.when(x == 3)
+        def _():
+            from_x(*t_line, 1).wait_recv()
+            from_x(*t_line, 2).wait_recv()
+            both = join(t_row[2], t_row[1])
+            for xx in range(NX - 1):
                 from_x(*l_line, xx).wait_recv()
-                row = l_row[xx].astype(F32)
-                if xx == 0:
-                    state[...] = row
-                else:
-                    from_x(*t_line, xx).wait_recv()
-                    held = state[...]
-                    state[...] = held + nn(t_row[xx], held.astype(BF16)) + row
+            state[...] = (
+                nn(both, l_row[0]) + nn(t_row[2], l_row[1])
+                + l_row[0].astype(F32) + l_row[1].astype(F32) + l_row[2].astype(F32)
+            )
 
         start = state[...]
         start_b = start.astype(BF16)
@@ -445,6 +466,40 @@
             @pl.when(z == zz)
             def _():
                 s_in[mine] = s_send[zz]
+
+    wait_exchange(2)
+
+    def outputs(c, carry):
+        rows = block_rows(c)
+        for j in range(HK):
+            qb = block(q_recv, c, slice(j * C, (j + 1) * C))
+            kb = block(k_recv, c, slice(j * C, (j + 1) * C))
+            qf = qb.astype(F32)
+            qc = lax.rsqrt(jnp.sum(qf * qf, 1, keepdims=True) + EPS) * (C ** -0.5)
+            scores = jnp.where(ri >= ci, nt(qb, kb) * qc * rk_row[j, c, 0:1, :], 0.0).astype(BF16)
+            unit = qf * qc
+            for n in (2 * j, 2 * j + 1):
+                part = nn(scores, wu[n, c])
+                eff = unit - part[:, :C]
+                moved = nn(eff.astype(BF16), before[n, c])
+                y_q[n, rows, :] = (eff + moved[:, :C]).astype(BF16)
+                y_o[n, rows, :] = part[:, C:] + moved[:, C:]
+        return carry
+
+    lax.fori_loop(0, NB, outputs, 0)
+
+    wait_exchange(3)
+    loads[6].wait()
+    gain = gain_in[...].astype(F32)
+
+    def gates(c, carry):
+        rows = block_rows(c)
+        for n in range(HV):
+            v = block(g_recv, c, slice(n * C, (n + 1) * C)).astype(F32)
+            gate[rows, n * C : (n + 1) * C] = v / (1.0 + jnp.exp(-v)) * gain
+        return carry
+
+    lax.fori_loop(0, NB, gates, 0)
 
     def to_sibling(n):
         cols = slice(n * C, (n + 1) * C)
@@ -475,21 +530,32 @@
         to_sibling(n).start()
 
     loads[5].wait()
-    weight_copy.wait_recv()
-    for n in range(HV):
-        to_sibling(n).wait_recv()
-
     tile, piece = 256, 512
 
-    def project(first):
+    def project(first, started):
         def one(t, carry):
             cols = pl.ds(pl.multiple_of(first + t * tile, tile), tile)
-            value = nn(g_mine[core], w_own[:, cols]) + nn(g_sib[...], w_sib[:, cols])
+            value = p_f[:, cols] if started else nn(g_mine[core], w_own[:, cols])
+            value = value + nn(g_sib[...], w_sib[:, cols])
             p_f[:, cols] = value
             p_b[:, cols] = value.astype(BF16)
             return carry
 
         lax.fori_loop(0, piece // tile, one, 0)
+
+    def begin(first):
+        def one(t, carry):
+            cols = pl.ds(pl.multiple_of(first + t * tile, tile), tile)
+            p_f[:, cols] = nn(g_mine[core], w_own[:, cols])
+            return carry
+
+        lax.fori_loop(0, piece // tile, one, 0)
+
+    begin(0)
+    begin(HALF)
+    weight_copy.wait_recv()
+    for n in range(HV):
+        to_sibling(n).wait_recv()
 
     def rows_of(dy):
         return pl.ds(pl.multiple_of(lax.rem(y + dy, NY) * ROWS, ROWS), ROWS)
@@ -511,9 +577,9 @@
     joins_b = [ring(8 + i, join_b.at[:, near[i]], plus_b.at[:, near[i]], 3) for i in range(2)]
     copies = relays_a + relays_b + [alone_a, alone_b] + joins_a + joins_b
     for i in range(2):
-        project(i * piece)
+        project(i * piece, i == 0)
         relays_a[i].start()
-        project(HALF + i * piece)
+        project(HALF + i * piece, i == 0)
         relays_b[i].start()
     alone_a.start()
     alone_b.start()
@@ -526,17 +592,20 @@
         joins_b[i].start()
     alone_a.wait_recv()
     alone_b.wait_recv()
+    stores = []
     for i in range(2):
-        joins_a[i].wait_recv()
-        out_ref[:, near[i]] = (
-            p_f[rows_of(0), near[i]] + minus_a[:, near[i]].astype(F32) + plus_a[:, near[i]].astype(F32)
-        ).astype(BF16)
-        joins_b[i].wait_recv()
-        out_ref[:, far[i]] = (
-            p_f[rows_of(0), far[i]] + minus_b[:, near[i]].astype(F32) + plus_b[:, near[i]].astype(F32)
-        ).astype(BF16)
-
-    for array in range(4):
+        for joins, cols, minus, plus in ((joins_a, near, minus_a, plus_a), (joins_b, far, minus_b, plus_b)):
+            joins[i].wait_recv()
+            out_v[:, cols[i]] = (
+                p_f[rows_of(0), cols[i]] + minus[:, near[i]].astype(F32) + plus[:, near[i]].astype(F32)
+            ).astype(BF16)
+            store = pltpu.make_async_copy(
+                out_v.at[:, cols[i]], out_hbm.at[:, cols[i]], out_sem.at[len(stores)]
+            )
+            store.start()
+            stores.append(store)
+
+    for array in range(1, 4):
         for i in range(len(peers)):
             peer_copy(array, i).wait_send()
     weight_copy.wait_send()
@@ -566,11 +635,12 @@
 
     for copy in copies:
         copy.wait_send()
+    for store in stores:
+        store.wait()
 
 
 def per_device(queries, key_vectors, value_vectors, output_gate, write_strength, norm_gain, output_weight):
     any_space = pl.BlockSpec(memory_space=pl.ANY)
-    vmem = pl.BlockSpec(memory_space=pltpu.VMEM)
     dma = pltpu.SemaphoreType.DMA
     v = pltpu.VMEM
     kh, vh = HK * NH, HV * NH
@@ -585,22 +655,23 @@
         v((HV, NB, C, C), BF16), v((HV, NB, C, C), F32), v((HV, NB, C, 2 * C), BF16), v((HV, NB, C, C), F32),
         v((HV, NB, C, 2 * C), BF16),
         v((HV, TOK, C), BF16), v((HV, TOK, C), F32), v((TOK, HV * C), F32),
-        v((HV, C, C), BF16), v((HV, C, C), BF16), v((NZ, C, C), BF16), v((NZ, C, C), BF16),
+        v((HV, C, C), BF16), v((HV, C, C), BF16), v((HV, C, C), BF16), v((NZ, C, C), BF16), v((NZ, C, C), BF16),
+        v((C, (NZ - 1) * C), BF16),
         v((3, 4 * C, C), BF16), v((NZ, C, C), BF16), v((NZ, C, C), F32), v((NX, C, C), BF16), v((NX, C, C), BF16),
         v((C, C), F32), v((NZ, C, C), BF16), v((HV, C, C), BF16),
         v((2, NY * ROWS, HV * C), BF16), v((NY * ROWS, HV * C), BF16),
         v((NY * ROWS, DM), F32), v((NY * ROWS, DM), BF16),
         half, half, half, half, half, half, half, half,
-        dma((6,)), dma((4,)), dma((4, 7)), dma((4, 7)), dma, dma,
+        dma((7,)), dma((4,)), dma((4, 7)), dma((4, 7)), dma, dma,
         dma((HV,)), dma((NZ,)), dma((HV,)), dma((NZ,)), dma((NX,)), dma((NX,)), dma((NX,)), dma((NX,)),
         dma((NZ,)), dma((HV,)),
-        dma((HV,)), dma((HV,)), dma((10,)), dma((10,)),
+        dma((HV,)), dma((HV,)), dma((10,)), dma((10,)), v((ROWS, DM), BF16), dma((4,)), v((1, C), BF16),
     ]
     return pl.pallas_call(
         kernel,
         out_shape=jax.ShapeDtypeStruct((ROWS, DM), BF16),
-        in_specs=[any_space] * 5 + [vmem, any_space],
-        out_specs=vmem,
+        in_specs=[any_space] * 7,
+        out_specs=any_space,
         scratch_shapes=scratch,
         compiler_params=pltpu.CompilerParams(
             collective_id=0, has_side_effects=True, vmem_limit_bytes=60 * 1024 * 1024

time: 54.5 us -> 52.6 us (0.965)
  Pallas kernels: 52.3 us -> 50.8 us
    pallas_call x1, Pallas kernels: 52.3 us -> 50.8 us  [per_device(): pl.pallas_call(kernel, out_shape=jax.ShapeDtypeStruct((ROWS, DM), BF16),...]
where the time goes in v3:
time: 52.6 us; the launch traced here: 52.5 us
  Pallas kernels  50.8 us (97%)
  local copies, waits for them, and re-layouts  1.67 us (3%)
    pallas_call x1, Pallas kernels, per_device(): pl.pallas_call(kernel, out_shape=jax.ShapeDtypeStruct((ROWS, DM), BF16),...  50.8 us
    unnamed x1, local copies, waits for them, and re-layouts  1.67 us

profile of v3, /device:TPU:5, one launch (start us, length us, event | category | flops | bytes accessed | tf_op | source)
XLA Modules:
  0.0 52.5 jit_solution(6553577736864144257)
XLA Ops:
  0.0 50.8 %shard_map.73 = bf16[64,2048]{1,0:T(8,128)(2,1)} custom-call(bf16[1024,128]{1,0:T(8,128)(2,1)} %bitcast.8, bf16[1024,128]{1,0:T(8,128)(2,1)} %bitcast.9, bf16[2048,128]{1,0:T(8,128)(2,1)} %bitcast.6, bf16[2048,128]{1,0:T(8,128)(2,1)} %bitcast.7, bf16[32,64]{1,0:T(8,128)(2,1)} %bitcast.10, bf16[1,128]{1,0:T(2,128)(2,1)} %bitcast.11, bf16[512,2048]{1,0:T(8,128)(2,1)} %w_hbm.1), custom_call_target="tpu_custom_call" | custom-call | tf_op jit(solution)/shard_map/pallas_call | solution.py:670
  50.8 1.7 %copy.9 = bf16[64,2048]{1,0:T(8,128)(2,1)} copy(bf16[64,2048]{1,0:T(8,128)(2,1)} %shard_map.73) | data formatting | bytes 524288

commit v4 on v3

--- a/solution.py
+++ b/solution.py
@@ -112,12 +112,13 @@
         return lax.rem(y + dy, NY) * 2 + lax.rem(core + dc, 2)
 
     barrier = pltpu.get_barrier_semaphore()
-    for dy, dc in peers:
-        pl.semaphore_signal(barrier, inc=1, device_id=on_head(head_at(dy, dc)), device_id_type=MESH)
-    for dz in range(1, NZ):
+    for dz in (4, 3, 5, 2, 6, 1, 7):
         pl.semaphore_signal(barrier, inc=1, device_id=on_z(lax.rem(z + dz, NZ)), device_id_type=MESH)
     for dx in range(1, NX):
         pl.semaphore_signal(barrier, inc=1, device_id=on_x(lax.rem(x + dx, NX)), device_id_type=MESH)
+
+    for dy, dc in peers:
+        pl.semaphore_signal(barrier, inc=1, device_id=on_head(head_at(dy, dc)), device_id_type=MESH)
 
     loads = [
         pltpu.make_async_copy(src, dst, in_sem.at[i])

time: 52.6 us -> 52.6 us (level)
  no operation moved by 1% of the time
where the time goes in v4:
time: 52.6 us; the launch traced here: 52.5 us
  Pallas kernels  50.8 us (97%)
  local copies, waits for them, and re-layouts  1.67 us (3%)
    pallas_call x1, Pallas kernels, per_device(): pl.pallas_call(kernel, out_shape=jax.ShapeDtypeStruct((ROWS, DM), BF16),...  50.8 us
    unnamed x1, local copies, waits for them, and re-layouts  1.67 us

profile of v4, /device:TPU:5, one launch (start us, length us, event | category | flops | bytes accessed | tf_op | source)
XLA Modules:
  0.0 52.5 jit_solution(1171344538595672314)
XLA Ops:
  0.0 50.8 %shard_map.73 = bf16[64,2048]{1,0:T(8,128)(2,1)} custom-call(bf16[1024,128]{1,0:T(8,128)(2,1)} %bitcast.8, bf16[1024,128]{1,0:T(8,128)(2,1)} %bitcast.9, bf16[2048,128]{1,0:T(8,128)(2,1)} %bitcast.6, bf16[2048,128]{1,0:T(8,128)(2,1)} %bitcast.7, bf16[32,64]{1,0:T(8,128)(2,1)} %bitcast.10, bf16[1,128]{1,0:T(2,128)(2,1)} %bitcast.11, bf16[512,2048]{1,0:T(8,128)(2,1)} %w_hbm.1), custom_call_target="tpu_custom_call" | custom-call | tf_op jit(solution)/shard_map/pallas_call | solution.py:671
  50.8 1.7 %copy.9 = bf16[64,2048]{1,0:T(8,128)(2,1)} copy(bf16[64,2048]{1,0:T(8,128)(2,1)} %shard_map.73) | data formatting | bytes 524288
